TPU v7x, 32 devices: a whole 2x2x4 slice. The times are simulated.
32 devices in a mesh: scalar: 4 (over z), space: 8 (over y, x, core).
Axes of the slice: x: 2, y: 2, z: 4, core: 2. Of those that a mesh axis runs over, the one named last changes fastest.
Arguments:
- scalars: float32 [16, 2, 1024, 1024], P('scalar', None, 'space'), may hold values from -6 to 6
- velocity_x: float32 [2, 1024, 1024], P(None, 'space', 'scalar'), may hold values from 0 to 1, as said below
- velocity_y: float32 [2, 1024, 1024], P(None, 'space', 'scalar'), may hold values from 0 to 1, as said below
- shift_x: int32 [2, 1024], P(None, 'space'), may hold values from -8 to 8
- shift_y: int32 [1024], P('space'), may hold values from -8 to 8
- schmidt: int32 [16], P('scalar'), may hold values from 1 to 5
Outputs:
- transported: float32 [16, 2, 1024, 1024], P('scalar', None, 'space')
Inputs may be any that keep to these rules, and one draw needn't show every extreme that they name: shift_x and shift_y are whole cells of displacement along the line; they act periodically. `velocity_x`: fractions of a cell. `velocity_y`: fractions of a cell.
All inputs are finite; a program needn't handle non-finite values.
Results may differ from a plain program's by a relative error of at most 0.0003.
Values sent between devices are 32-bit elements; how exact they have to be, the bound alone decides.
A program may use at most 192 MiB of HBM per device.

v0:
```python
import math
import jax
import jax.numpy as jnp
from jax import lax
from jax.sharding import PartitionSpec as P

NY = 1024


def spline(distance):
    magnitude = jnp.abs(distance)
    far_part = jnp.maximum(3.0 - magnitude, 0.0)
    middle = jnp.maximum(2.0 - magnitude, 0.0)
    near_part = jnp.maximum(1.0 - magnitude, 0.0)
    return (far_part**5 - 6.0 * middle**5 + 15.0 * near_part**5) / 120.0


def remesh(fields, fraction, shift_line):
    summed = jnp.zeros_like(fields)
    for offset in range(-2, 4):
        weight = spline(offset - fraction)
        summed = summed + jnp.roll(fields * weight, offset, axis=-1)
    line_shift = shift_line[None, :, :, None]
    moved = summed
    for amount in range(-8, 9):
        moved = jnp.where(line_shift == amount, jnp.roll(summed, amount, axis=-1), moved)
    return moved


def remesh_columns(fields, fraction, shift_cols):
    summed = jnp.zeros_like(fields)
    for offset in range(-2, 4):
        weight = spline(offset - fraction)
        summed = summed + jnp.roll(fields * weight[None], offset, axis=2)
    column_shift = shift_cols[None, None, None, :]
    moved = summed
    for amount in range(-8, 9):
        moved = jnp.where(column_shift == amount, jnp.roll(summed, amount, axis=2), moved)
    return moved


def spectral_tables(length):
    midpoint = length // 2
    column = jnp.arange(length, dtype=jnp.int32)
    wavenum = jnp.where(column <= midpoint, column, column - midpoint)
    phases = column[:, None] * wavenum[None, :] % length
    angles = phases.astype(jnp.float32) * (2.0 * math.pi / length)
    forward = jnp.where((column <= midpoint)[None, :], jnp.cos(angles), jnp.sin(angles))
    inverse_weight = jnp.where((wavenum == 0) | (column == midpoint), 1.0, 2.0) / length
    inverse = forward.T * inverse_weight[:, None]
    relative = wavenum.astype(jnp.float32) / midpoint
    return (forward, inverse, relative * relative)


def diffuse(fields, diffusivity, tables):
    forward, inverse, wave_square = tables
    initial = fields.shape
    rows_flat = fields.reshape(-1, initial[-1])
    spectra = jnp.dot(
        rows_flat, forward, precision=lax.Precision.HIGHEST, preferred_element_type=jnp.float32
    )
    damping = jnp.exp(-diffusivity[:, None] * wave_square[None, :])
    spectra = spectra.reshape(initial) * damping[:, None, None, :]
    result = jnp.dot(
        spectra.reshape(-1, initial[-1]),
        inverse,
        precision=lax.Precision.HIGHEST,
        preferred_element_type=jnp.float32,
    )
    return result.reshape(initial)


def diffuse_columns(fields, diffusivity, tables):
    forward, inverse, wave_square = tables
    spectra = jnp.einsum(
        "jk,szjx->szkx",
        forward,
        fields,
        precision=lax.Precision.HIGHEST,
        preferred_element_type=jnp.float32,
    )
    damping = jnp.exp(-diffusivity[:, None] * wave_square[None, :])
    spectra = spectra * damping[:, None, :, None]
    return jnp.einsum(
        "kj,szkx->szjx",
        inverse,
        spectra,
        precision=lax.Precision.HIGHEST,
        preferred_element_type=jnp.float32,
    )


def one_sweep(fields, fraction, shift_line, diffusivity, tables):
    return diffuse(remesh(fields, fraction, shift_line), diffusivity, tables)


def fetch_velocity(velocity_x):
    return lax.all_gather(velocity_x, "scalar", axis=2, tiled=True)


def on_device(scalars, velocity_x, velocity_y, shift_x, shift_y, schmidt):
    diffusivity = jnp.exp2((3 - schmidt).astype(jnp.float32))
    tables_x = spectral_tables(scalars.shape[3])
    tables_y = spectral_tables(NY)
    along_x = fetch_velocity(velocity_x)
    fields = one_sweep(scalars, along_x, shift_x, 0.5 * diffusivity, tables_x)
    along_y = lax.all_gather(velocity_y, "scalar", axis=2, tiled=True)
    fields_cols, velocity_cols = (
        lax.all_to_all(fields, "space", split_axis=3, concat_axis=2, tiled=True),
        lax.all_to_all(along_y[None], "space", split_axis=3, concat_axis=2, tiled=True),
    )
    remeshed = remesh_columns(fields_cols, velocity_cols[0], shift_y)
    returned = diffuse_columns(remeshed, diffusivity, tables_y)
    fields = lax.all_to_all(returned, "space", split_axis=2, concat_axis=3, tiled=True)
    along_x = fetch_velocity(velocity_x)
    return one_sweep(fields, along_x, shift_x, 0.5 * diffusivity, tables_x)


def solution(mesh):
    return jax.shard_map(
        on_device,
        mesh=mesh,
        in_specs=(
            P("scalar", None, "space", None),
            P(None, "space", "scalar"),
            P(None, "space", "scalar"),
            P(None, "space"),
            P("space"),
            P("scalar"),
        ),
        out_specs=P("scalar", None, "space", None),
        check_vma=False,
    )
```

profile of v0, /device:TPU:0, one launch (start us, length us, event | category | flops | bytes accessed | tf_op | source)
XLA Modules:
  0.0 669.2 jit_solution(6938982422818095112)
XLA Ops:
  13.6 26.0 %all-gather.3.cloned.1.call-done = f32[2,128,1024]{2,1,0:T(8,128)} async-done(((f32[2,128,256]{2,1,0:T(8,128)}), f32[2,128,1024]{2,1,0:T(8,128)}) %all-gather.3.cloned.1.call-update) | async-done | bytes 1048592 | tf_op jit(solution)/shard_map/all_gather | solution.py:98
  39.6 6.5 add_multiply_fusion.9
  46.1 6.2 broadcast_multiply_fusion.1
  59.4 8.0 %fusion.9 = f32[4,2,128,1024]{3,2,1,0:T(8,128)S(1)} fusion(f32[4,2,128,2]{3,2,1,0:T(8,128)S(1)} %slice.569, f32[4,2,128,1022]{3,2,1,0:T(8,128)} %slice.568, f32[4,2,128,1]{3,2,1,0:T(8,128)S(1)} %slice.571, f32[4,2,128,1023]{3,2,1,0:T(8,128)} %slice.570, f32[4,2,128,1023]{3,2,1,0:T(8,128)S(1)} %bitcast.156, f32[4,2,128,1]{3,2,1,0:T(8,128)S(1)} %slice.572, ...), kind=kLoop, calls=%fused_computation.16 | loop fusion | flops 11534336 | bytes 30408704 | tf_op jit(solution)/shard_map/add | solution.py:22
  108.0 5.1 fusion.270
  116.9 26.6 %maximum_select_fusion.99 = f32[4,2,128,1024]{3,2,1,0:T(8,128)S(1)} fusion(f32[4,2,128,1016]{3,2,1,0:T(8,128)} %get-tuple-element.80, f32[4,2,128,8]{3,2,1,0:T(8,128)} %get-tuple-element.82, f32[4,2,128,1017]{3,2,1,0:T(8,128)} %get-tuple-element.84, f32[4,2,128,7]{3,2,1,0:T(8,128)} %get-tuple-element.86, ...), kind=kLoop, calls=%fused_computation.17.clone.clone.2 | loop fusion | flops 34603008 | bytes 75501824 | tf_op jit(solution)/shard_map/dot_general | solution.py:59
  143.6 32.3 %fusion.10 = f32[4,2,128,1024]{3,2,1,0:T(8,128)S(1)} fusion(s32[1024]{0:T(1024)S(1)} %copy-done.64, pred[1024]{0:T(1024)(128)(4,1)S(1)} %copy-done.67, f32[4,2,128,1024]{3,2,1,0:T(8,128)S(1)} %maximum_select_fusion.99), kind=kOutput, calls=%fused_computation.18 | convolution fusion | flops 12900630528 | bytes 8393728 | tf_op jit(solution)/shard_map/dot_general | solution.py:59
  176.8 32.3 %fusion.127 = f32[4,2,128,1024]{3,2,1,0:T(8,128)} fusion(f32[1024]{0:T(1024)S(1)} %copy-done.65, s32[1024]{0:T(1024)S(1)} %copy-done.64, pred[1024]{0:T(1024)(128)(4,1)S(1)} %copy-done.67, f32[4,2,128,1024]{3,2,1,0:T(8,128)S(1)} %fusion.301), kind=kOutput, calls=%fused_computation.181 | convolution fusion | flops 12901679104 | bytes 8397824 | tf_op jit(solution)/shard_map/dot_general | solution.py:64
  209.2 7.2 %copy.92 = f32[4,2,128,1024]{2,1,0,3:T(2,128)} copy(f32[4,2,128,1024]{3,2,1,0:T(8,128)} %fusion.127) | data formatting | bytes 8388608 | tf_op jit(solution)/shard_map/dot_general | solution.py:64
  221.1 6.2 subtract_maximum_fusion.11
  278.0 5.0 copy.93
  283.0 5.3 copy.94
  288.3 6.2 bitcast_multiply_fusion
  331.8 17.1 %maximum_select_fusion.100 = f32[4,2,1024,128]{3,2,1,0:T(8,128)S(1)} fusion(f32[4,2,1016,128]{3,2,1,0:T(8,128)} %get-tuple-element.43, f32[4,2,8,128]{3,2,1,0:T(8,128)S(1)} %get-tuple-element.45, f32[4,2,1017,128]{3,2,1,0:T(8,128)S(1)} %get-tuple-element.47, f32[4,2,7,128]{3,2,1,0:T(8,128)S(1)} %get-tuple-element.49, ...), kind=kLoop, calls=%fused_computation.72.clone.clone.2 | loop fusion | flops 34603008 | bytes 75499648 | tf_op jit(solution)/shard_map/jk,szjx->szkx/dot_general | solution.py:75
  348.9 44.4 %fusion.49 = f32[4,2,128,1024]{3,2,1,0:T(8,128)S(1)} fusion(s32[1024]{0:T(1024)S(1)} %copy-done.64, pred[1024]{0:T(1024)(128)(4,1)S(1)} %copy-done.67, f32[4,2,1024,128]{3,2,1,0:T(8,128)S(1)} %maximum_select_fusion.100), kind=kOutput, calls=%fused_computation.73 | convolution fusion | flops 12900630528 | bytes 8393728 | tf_op jit(solution)/shard_map/jk,szjx->szkx/dot_general | solution.py:75
  394.2 32.3 %fusion.142 = f32[4,2,1024,128]{2,3,1,0:T(8,128)} fusion(f32[1024]{0:T(1024)S(1)} %copy-done.65, s32[1024]{0:T(1024)S(1)} %copy-done.64, pred[1024]{0:T(1024)(128)(4,1)S(1)} %copy-done.67, f32[4,2,1024,128]{2,3,1,0:T(8,128)S(1)} %fusion.303), kind=kOutput, calls=%fused_computation.204 | convolution fusion | flops 12901679104 | bytes 8397824 | tf_op jit(solution)/shard_map/kj,szkx->szjx/dot_general | solution.py:84
  426.5 7.2 %copy.122 = f32[4,2,1024,128]{3,1,0,2:T(2,128)} copy(f32[4,2,1024,128]{2,3,1,0:T(8,128)} %fusion.142) | data formatting | bytes 8388608 | tf_op jit(solution)/shard_map/kj,szkx->szjx/transpose | solution.py:84
  433.8 53.2 %all_to_all.45 = f32[4,2,1024,128]{3,1,0,2:T(2,128)S(1)} all-to-all(f32[4,2,1024,128]{3,1,0,2:T(2,128)} %copy.122), channel_id=1, replica_groups=mesh['scalar'=4,'space'=8] {'space'}, dimensions={2} | all-to-all | bytes 8388608 | tf_op jit(solution)/shard_map/all_to_all | solution.py:114
  496.4 5.6 broadcast_multiply_fusion
  512.3 8.3 %fusion.87 = f32[4,2,128,1024]{3,2,1,0:T(8,128)S(1)} fusion(f32[4,2,128,2]{3,2,1,0:T(8,128)} %slice.653, f32[4,2,128,1022]{3,2,1,0:T(8,128)} %slice.652, f32[4,2,128,1]{3,2,1,0:T(8,128)} %slice.655, f32[4,2,128,1023]{3,2,1,0:T(8,128)} %slice.654, f32[4,2,128,1023]{3,2,1,0:T(8,128)} %bitcast.154, f32[4,2,128,1]{3,2,1,0:T(8,128)S(1)} %slice.656, ...), kind=kLoop, calls=%fused_computation.126 | loop fusion | flops 11534336 | bytes 30408704 | tf_op jit(solution)/shard_map/add | solution.py:22
  553.7 5.0 fusion.230
  567.6 27.1 %maximum_select_fusion.101 = f32[4,2,128,1024]{3,2,1,0:T(8,128)} fusion(f32[4,2,128,1016]{3,2,1,0:T(8,128)} %get-tuple-element.6, f32[4,2,128,8]{3,2,1,0:T(8,128)} %get-tuple-element.8, f32[4,2,128,1017]{3,2,1,0:T(8,128)} %get-tuple-element.10, f32[4,2,128,7]{3,2,1,0:T(8,128)S(1)} %get-tuple-element.12, ...), kind=kLoop, calls=%fused_computation.127.clone.clone | loop fusion | flops 34603008 | bytes 75501824 | tf_op jit(solution)/shard_map/dot_general | solution.py:59
  594.7 34.5 %fusion.88 = f32[4,2,128,1024]{3,2,1,0:T(8,128)S(1)} fusion(s32[1024]{0:T(1024)S(1)} %copy-done.64, pred[1024]{0:T(1024)(128)(4,1)S(1)} %copy-done.67, f32[4,2,128,1024]{3,2,1,0:T(8,128)} %maximum_select_fusion.101), kind=kOutput, calls=%fused_computation.128 | convolution fusion | flops 12900630528 | bytes 8393728 | tf_op jit(solution)/shard_map/dot_general | solution.py:59
  630.2 32.0 %fusion.123 = f32[4,2,128,1024]{3,2,1,0:T(8,128)} fusion(f32[1024]{0:T(1024)S(1)} %copy-done.65, s32[1024]{0:T(1024)S(1)} %copy-done.64, pred[1024]{0:T(1024)(128)(4,1)S(1)} %copy-done.67, f32[4,2,128,1024]{3,2,1,0:T(8,128)S(1)} %fusion.299), kind=kOutput, calls=%fused_computation.177 | convolution fusion | flops 12901679104 | bytes 8397824 | tf_op jit(solution)/shard_map/dot_general | solution.py:64
  (249 shorter events, 214.7 us)
Async XLA Ops:
  6.5 33.1 %all-gather.3.cloned.1.call-start = ((), (), s32[]{:S(2)}) async-start(), calls=%async_computation.3 | async-start | bytes 1310720 | tf_op jit(solution)/shard_map/all_gather | solution.py:98
  7.3 105.9 %all-gather.5.cloned.1.call-start = ((), (), s32[]{:S(2)}) async-start(), calls=%async_computation.4 | async-start | bytes 1310720 | tf_op jit(solution)/shard_map/all_gather | solution.py:107
  12.1 104.6 %copy-start.30 = (pred[2,128]{1,0:T(4,128)(4,1)}, pred[2,128]{1,0:T(4,128)(4,1)S(1)}, u32[]{:S(2)}) copy-start(pred[2,128]{1,0:T(4,128)(4,1)S(1)} %get-tuple-element.142) | copy-start | bytes 772
  12.1 104.6 %copy-start.32 = (pred[2,128]{1,0:T(4,128)(4,1)}, pred[2,128]{1,0:T(4,128)(4,1)S(1)}, u32[]{:S(2)}) copy-start(pred[2,128]{1,0:T(4,128)(4,1)S(1)} %get-tuple-element.143) | copy-start | bytes 772
  12.1 104.6 %copy-start.34 = (pred[2,128]{1,0:T(4,128)(4,1)}, pred[2,128]{1,0:T(4,128)(4,1)S(1)}, u32[]{:S(2)}) copy-start(pred[2,128]{1,0:T(4,128)(4,1)S(1)} %get-tuple-element.144) | copy-start | bytes 772
  12.1 104.6 %copy-start.36 = (pred[2,128]{1,0:T(4,128)(4,1)}, pred[2,128]{1,0:T(4,128)(4,1)S(1)}, u32[]{:S(2)}) copy-start(pred[2,128]{1,0:T(4,128)(4,1)S(1)} %get-tuple-element.145) | copy-start | bytes 772
  12.1 104.6 %copy-start.38 = (pred[2,128]{1,0:T(4,128)(4,1)}, pred[2,128]{1,0:T(4,128)(4,1)S(1)}, u32[]{:S(2)}) copy-start(pred[2,128]{1,0:T(4,128)(4,1)S(1)} %get-tuple-element.146) | copy-start | bytes 772
  12.2 104.6 %copy-start.40 = (pred[2,128]{1,0:T(4,128)(4,1)}, pred[2,128]{1,0:T(4,128)(4,1)S(1)}, u32[]{:S(2)}) copy-start(pred[2,128]{1,0:T(4,128)(4,1)S(1)} %get-tuple-element.147) | copy-start | bytes 772
  12.2 104.6 %copy-start.42 = (pred[2,128]{1,0:T(4,128)(4,1)}, pred[2,128]{1,0:T(4,128)(4,1)S(1)}, u32[]{:S(2)}) copy-start(pred[2,128]{1,0:T(4,128)(4,1)S(1)} %get-tuple-element.148) | copy-start | bytes 772
  12.2 104.6 %copy-start.44 = (pred[2,128]{1,0:T(4,128)(4,1)}, pred[2,128]{1,0:T(4,128)(4,1)S(1)}, u32[]{:S(2)}) copy-start(pred[2,128]{1,0:T(4,128)(4,1)S(1)} %get-tuple-element.149) | copy-start | bytes 772
  12.2 104.6 %copy-start.46 = (pred[2,128]{1,0:T(4,128)(4,1)}, pred[2,128]{1,0:T(4,128)(4,1)S(1)}, u32[]{:S(2)}) copy-start(pred[2,128]{1,0:T(4,128)(4,1)S(1)} %get-tuple-element.150) | copy-start | bytes 772
  12.2 104.6 %copy-start.48 = (pred[2,128]{1,0:T(4,128)(4,1)}, pred[2,128]{1,0:T(4,128)(4,1)S(1)}, u32[]{:S(2)}) copy-start(pred[2,128]{1,0:T(4,128)(4,1)S(1)} %get-tuple-element.151) | copy-start | bytes 772
  12.2 104.6 %copy-start.50 = (pred[2,128]{1,0:T(4,128)(4,1)}, pred[2,128]{1,0:T(4,128)(4,1)S(1)}, u32[]{:S(2)}) copy-start(pred[2,128]{1,0:T(4,128)(4,1)S(1)} %get-tuple-element.152) | copy-start | bytes 772
  12.2 104.6 %copy-start.52 = (pred[2,128]{1,0:T(4,128)(4,1)}, pred[2,128]{1,0:T(4,128)(4,1)S(1)}, u32[]{:S(2)}) copy-start(pred[2,128]{1,0:T(4,128)(4,1)S(1)} %get-tuple-element.153) | copy-start | bytes 772
  12.2 104.6 %copy-start.54 = (pred[2,128]{1,0:T(4,128)(4,1)}, pred[2,128]{1,0:T(4,128)(4,1)S(1)}, u32[]{:S(2)}) copy-start(pred[2,128]{1,0:T(4,128)(4,1)S(1)} %get-tuple-element.154) | copy-start | bytes 772
  13.6 162.3 %copy-start.27 = (f32[4,1024]{1,0:T(4,128)}, f32[4,1024]{1,0:T(4,128)S(1)}, u32[]{:S(2)}) copy-start(f32[4,1024]{1,0:T(4,128)S(1)} %get-tuple-element.141) | copy-start | bytes 49156
  46.1 13.3 %copy-start.4 = (f32[2,128,1024]{2,1,0:T(8,128)}, f32[2,128,1024]{2,1,0:T(8,128)S(1)}, u32[]{:S(2)}) copy-start(f32[2,128,1024]{2,1,0:T(8,128)S(1)} %get-tuple-element.134) | copy-start | bytes 3145732
  67.5 40.6 %copy-start = (f32[4,2,128,1024]{3,2,1,0:T(8,128)}, f32[4,2,128,1024]{3,2,1,0:T(8,128)S(1)}, u32[]{:S(2)}) copy-start(f32[4,2,128,1024]{3,2,1,0:T(8,128)S(1)} %fusion.9) | copy-start | bytes 12582916
  113.1 103.3 %all-to-all-start.1 = ((f32[1,2,128,1024]{2,1,0,3:T(2,128)}), f32[1,2,128,1024]{2,1,0,3:T(2,128)S(1)}, u32[]{:S(2)}, u32[]{:S(2)}) async-start(f32[1,2,128,1024]{2,1,0,3:T(2,128)} %bitcast.199), calls=%async_computation.1 | async-start | bytes 2097152 | tf_op jit(solution)/shard_map/all_to_all | solution.py:110
  116.9 26.7 %copy-start.64 = (s32[1024]{0:T(1024)S(1)}, s32[1024]{0:T(1024)}, u32[]{:S(2)}) copy-start(s32[1024]{0:T(1024)} %add_select_fusion.2) | copy-start | bytes 12292
  116.9 26.7 %copy-start.67 = (pred[1024]{0:T(1024)(128)(4,1)S(1)}, pred[1024]{0:T(1024)(128)(4,1)}, u32[]{:S(2)}) copy-start(pred[1024]{0:T(1024)(128)(4,1)} %iota_compare_fusion.1) | copy-start | bytes 3076
  216.4 61.6 %all-to-all-start = ((f32[4,2,128,1024]{2,1,0,3:T(2,128)}), f32[4,2,128,1024]{2,1,0,3:T(2,128)}, u32[]{:S(2)}, u32[]{:S(2)}) async-start(f32[4,2,128,1024]{2,1,0,3:T(2,128)} %copy.92), calls=%async_computation | async-start | bytes 8388608 | tf_op jit(solution)/shard_map/all_to_all | solution.py:109
  348.9 44.4 %copy-start.29 = (f32[4,1024]{1,0:T(4,128)S(1)}, f32[4,1024]{1,0:T(4,128)}, u32[]{:S(2)}) copy-start(f32[4,1024]{1,0:T(4,128)} %get-tuple-element.140) | copy-start | bytes 49156
  594.7 34.6 %copy-start.28 = (f32[4,1024]{1,0:T(4,128)S(1)}, f32[4,1024]{1,0:T(4,128)}, u32[]{:S(2)}) copy-start(f32[4,1024]{1,0:T(4,128)} %copy-done.27) | copy-start | bytes 49156
  (48 other events, 241.8 us)
Sparse Core Ops, SparseCore 0:
  8.9 30.6 all-gather.2
  41.2 27.4 all-gather.4
where the time goes:
time: 677 us; the launch traced here: 669 us
  local copies, waits for them, and re-layouts  219 us (32%)
  matrix products  208 us (31%)
  other arithmetic  139 us (21%)
  blocking collectives  53.2 us (8%)
  waiting for transfers between devices  26.7 us (4%)
  between operations  14.6 us (2%)
  starting transfers between devices  8.36 us (1%)
    slice x32, local copies, waits for them, and re-layouts, remesh(): jnp.roll(summed, amount, axis=-1)  92.3 us
    dot_general x2, matrix products, diffuse(): jnp.dot(rows_flat, forward, precision=lax.Precision.HIGHEST, preferred_el...  66.9 us
    dot_general x2, matrix products, diffuse(): jnp.dot(spectra.reshape(-1, initial[-1]), inverse, precision=lax.Precisio...  64.3 us
    dot_general x2, other arithmetic, diffuse(): jnp.dot(rows_flat, forward, precision=lax.Precision.HIGHEST, preferred_el...  53.8 us
    all_to_all x1, blocking collectives, on_device(): lax.all_to_all(returned, 'space', split_axis=2, concat_axis=3, tiled=True)  53.2 us
    dot_general x1, matrix products, diffuse_columns(): jnp.einsum('jk,szjx->szkx', forward, fields, precision=lax.Precision.HIGH...  44.4 us
    dot_general x1, matrix products, diffuse_columns(): jnp.einsum('kj,szkx->szjx', inverse, spectra, precision=lax.Precision.HIG...  32.3 us
    all_gather x1, waiting for transfers between devices, fetch_velocity(): return lax.all_gather(velocity_x, 'scalar', axis=2, tiled=True)  26 us
  transfers between devices with their start and end apart: 4, of which 1 were waited for; matrix products, arithmetic and copies ran while one was open for 35% of the time, Pallas kernels for 0%

commit v1 on v0

--- a/solution.py
+++ b/solution.py
@@ -111,7 +111,12 @@
     )
     remeshed = remesh_columns(fields_cols, velocity_cols[0], shift_y)
     returned = diffuse_columns(remeshed, diffusivity, tables_y)
-    fields = lax.all_to_all(returned, "space", split_axis=2, concat_axis=3, tiled=True)
+    fields = jnp.concatenate(
+        lax.all_to_all(
+            jnp.stack(jnp.split(returned, lax.axis_size("space"), axis=2)), "space", 0, 0
+        ),
+        axis=3,
+    )
     along_x = fetch_velocity(velocity_x)
     return one_sweep(fields, along_x, shift_x, 0.5 * diffusivity, tables_x)
 

time: 677 us -> 645 us (0.953)
  local copies, waits for them, and re-layouts: 219 us -> 178 us
  matrix products: 208 us -> 240 us
  other arithmetic: 139 us -> 118 us
    slice x32, local copies, waits for them, and re-layouts: 92.3 us -> 57.2 us  [remesh(): jnp.roll(summed, amount, axis=-1)]
    dot_general x2, matrix products: 66.9 us -> 88.2 us  [diffuse(): jnp.dot(rows_flat, forward, precision=lax.Precision.HIGHEST, preferred_el...]
    dot_general x2, other arithmetic: 53.8 us -> 39.6 us  [diffuse(): jnp.dot(rows_flat, forward, precision=lax.Precision.HIGHEST, preferred_el...]
    dot_general x2, matrix products: 64.3 us -> 75.3 us  [diffuse(): jnp.dot(spectra.reshape(-1, initial[-1]), inverse, precision=lax.Precisio...]
    all_to_all x2 -> x0, local copies, waits for them, and re-layouts: 9.43 us -> none  [on_device(): lax.all_to_all(returned, 'space', split_axis=2, concat_axis=3, tiled=True)]
    unnamed x137 -> x159, local copies, waits for them, and re-layouts: 5.26 us -> 14.5 us
    div x0 -> x6, local copies, waits for them, and re-layouts: none -> 8.44 us  [spline(): return (far_part ** 5 - 6.0 * middle ** 5 + 15.0 * near_part ** 5) / 120.0]
    slice x14, local copies, waits for them, and re-layouts: 17.5 us -> 9.61 us  [remesh(): summed = summed + jnp.roll(fields * weight, offset, axis=-1)]
  transfers between devices with their start and end apart: 4 -> 4, of which waited for: 1 -> 1; matrix products, arithmetic and copies ran while one was open for 35% -> 39% of each run, Pallas kernels for 0% -> 0%
where the time goes in v1:
time: 645 us; the launch traced here: 635 us
  matrix products  240 us (37%)
  local copies, waits for them, and re-layouts  178 us (28%)
  other arithmetic  118 us (18%)
  blocking collectives  53 us (8%)
  waiting for transfers between devices  22.7 us (4%)
  between operations  15.1 us (2%)
  starting transfers between devices  8.67 us (1%)
    dot_general x2, matrix products, diffuse(): jnp.dot(rows_flat, forward, precision=lax.Precision.HIGHEST, preferred_el...  88.2 us
    dot_general x2, matrix products, diffuse(): jnp.dot(spectra.reshape(-1, initial[-1]), inverse, precision=lax.Precisio...  75.3 us
    slice x32, local copies, waits for them, and re-layouts, remesh(): jnp.roll(summed, amount, axis=-1)  57.2 us
    all_to_all x1, blocking collectives, on_device(): lax.all_to_all(jnp.stack(jnp.split(returned, lax.axis_size('space'), axis...  53 us
    dot_general x1, matrix products, diffuse_columns(): jnp.einsum('jk,szjx->szkx', forward, fields, precision=lax.Precision.HIGH...  44.4 us
    dot_general x2, other arithmetic, diffuse(): jnp.dot(rows_flat, forward, precision=lax.Precision.HIGHEST, preferred_el...  39.6 us
    dot_general x1, matrix products, diffuse_columns(): jnp.einsum('kj,szkx->szjx', inverse, spectra, precision=lax.Precision.HIG...  31.8 us
    slice x16, local copies, waits for them, and re-layouts, remesh_columns(): jnp.roll(summed, amount, axis=2)  25.1 us
  transfers between devices with their start and end apart: 4, of which 1 were waited for; matrix products, arithmetic and copies ran while one was open for 39% of the time, Pallas kernels for 0%

profile of v1, /device:TPU:0, one launch (start us, length us, event | category | flops | bytes accessed | tf_op | source)
XLA Modules:
  0.0 634.7 jit_solution(10796203269827567171)
XLA Ops:
  10.8 5.4 copy.144
  17.6 22.0 %all-gather.3.cloned.1.call-done = f32[2,128,1024]{2,1,0:T(8,128)} async-done(((f32[2,128,256]{2,1,0:T(8,128)}), f32[2,128,1024]{2,1,0:T(8,128)}) %all-gather.3.cloned.1.call-update) | async-done | bytes 1048592 | tf_op jit(solution)/shard_map/all_gather | solution.py:98
  39.6 6.7 %add_multiply_fusion.9 = (f32[2,128,1024]{2,1,0:T(8,128)}, f32[2,128,1024]{2,1,0:T(8,128)}, f32[2,128,1024]{2,1,0:T(8,128)}, f32[2,128,1024]{2,1,0:T(8,128)}, f3...) fusion(f32[2,128,1024]{2,1,0:T(8,128)} %all-gather.3.cloned.1.call-done), kind=kLoop, calls=%fused_computation.303 | loop fusion | flops 34603008 | bytes 7340032 | tf_op jit(solution)/shard_map/div | solution.py:15
  66.1 9.6 %fusion.9 = f32[4,2,128,1024]{2,3,1,0:T(8,128)S(1)} fusion(f32[4,2,128,2]{2,3,1,0:T(2,128)S(1)} %slice.569, f32[4,2,128,1022]{2,3,1,0:T(8,128)} %slice.568, f32[4,2,128,1]{2,3,1,0:T(1,128)S(1)} %slice.571, f32[4,2,128,1023]{2,3,1,0:T(8,128)} %slice.570, f32[4,2,128,1023]{2,3,1,0:T(8,128)} %bitcast.197, f32[4,2,128,1]{2,3,1,0:T(1,128)S(1)} %slice.572, ...), kind=kLoop, calls=%fused_computation.16 | loop fusion | flops 11534336 | bytes 30408704 | tf_op jit(solution)/shard_map/add | solution.py:22
  75.7 4.4 fusion.280
  112.1 22.5 %maximum_select_fusion.99 = f32[4,2,128,1024]{2,3,1,0:T(8,128)S(1)} fusion(f32[4,2,128,1016]{2,3,1,0:T(8,128)} %get-tuple-element.80, f32[4,2,128,8]{2,3,1,0:T(8,128)S(1)} %get-tuple-element.82, f32[4,2,128,1017]{2,3,1,0:T(8,128)} %get-tuple-element.84, f32[4,2,128,7]{2,3,1,0:T(8,128)S(1)} %get-tuple-element.86, ...), kind=kLoop, calls=%fused_computation.17.clone.clone.2 | loop fusion | flops 34603008 | bytes 75501824 | tf_op jit(solution)/shard_map/dot_general | solution.py:59
  134.6 44.0 %fusion.10 = f32[4,2,128,1024]{3,2,1,0:T(8,128)S(1)} fusion(s32[1024]{0:T(1024)S(1)} %copy-done.69, pred[1024]{0:T(1024)(128)(4,1)S(1)} %copy-done.74, f32[4,2,128,1024]{2,3,1,0:T(8,128)S(1)} %maximum_select_fusion.99), kind=kOutput, calls=%fused_computation.18 | convolution fusion | flops 12900630528 | bytes 8393728 | tf_op jit(solution)/shard_map/dot_general | solution.py:59
  179.5 43.3 %fusion.127 = f32[4,2,128,1024]{3,2,1,0:T(8,128)} fusion(f32[1024]{0:T(1024)S(1)} %copy-done.70, s32[1024]{0:T(1024)S(1)} %copy-done.69, pred[1024]{0:T(1024)(128)(4,1)S(1)} %copy-done.74, f32[4,2,128,1024]{3,2,1,0:T(8,128)S(1)} %fusion.309), kind=kOutput, calls=%fused_computation.181 | convolution fusion | flops 12901679104 | bytes 8397824 | tf_op jit(solution)/shard_map/dot_general | solution.py:64
  222.8 7.2 %copy.156 = f32[4,2,128,1024]{2,1,0,3:T(2,128)} copy(f32[4,2,128,1024]{3,2,1,0:T(8,128)} %fusion.127) | data formatting | bytes 8388608 | tf_op jit(solution)/shard_map/dot_general | solution.py:64
  230.1 4.7 all-to-all-start
  234.8 6.3 subtract_maximum_fusion.11
  291.7 5.0 copy.157
  296.7 5.4 copy.158
  302.1 4.9 bitcast_multiply_fusion.6
  313.1 4.7 fusion.48
  342.9 17.1 %maximum_select_fusion.100 = f32[4,2,1024,128]{3,2,1,0:T(8,128)S(1)} fusion(f32[4,2,1016,128]{3,2,1,0:T(8,128)} %get-tuple-element.43, f32[4,2,8,128]{3,2,1,0:T(8,128)S(1)} %get-tuple-element.45, f32[4,2,1017,128]{3,2,1,0:T(8,128)S(1)} %get-tuple-element.47, f32[4,2,7,128]{3,2,1,0:T(8,128)S(1)} %get-tuple-element.49, ...), kind=kLoop, calls=%fused_computation.72.clone.clone.2 | loop fusion | flops 34603008 | bytes 75499648 | tf_op jit(solution)/shard_map/jk,szjx->szkx/dot_general | solution.py:75
  360.0 44.4 %fusion.49 = f32[4,2,128,1024]{3,2,1,0:T(8,128)S(1)} fusion(s32[1024]{0:T(1024)S(1)} %copy-done.69, pred[1024]{0:T(1024)(128)(4,1)S(1)} %copy-done.74, f32[4,2,1024,128]{3,2,1,0:T(8,128)S(1)} %maximum_select_fusion.100), kind=kOutput, calls=%fused_computation.73 | convolution fusion | flops 12900630528 | bytes 8393728 | tf_op jit(solution)/shard_map/jk,szjx->szkx/dot_general | solution.py:75
  405.3 31.8 %fusion.142 = f32[4,2,1024,128]{2,3,1,0:T(8,128)S(1)} fusion(f32[1024]{0:T(1024)S(1)} %copy-done.70, s32[1024]{0:T(1024)S(1)} %copy-done.69, pred[1024]{0:T(1024)(128)(4,1)S(1)} %copy-done.74, f32[4,2,1024,128]{2,3,1,0:T(8,128)S(1)} %fusion.311), kind=kOutput, calls=%fused_computation.210 | convolution fusion | flops 12901679104 | bytes 8397824 | tf_op jit(solution)/shard_map/kj,szkx->szjx/dot_general | solution.py:84
  437.8 53.0 %all_to_all.32 = f32[8,4,2,128,128]{3,4,2,1,0:T(8,128)S(1)} all-to-all(f32[8,4,2,128,128]{3,4,2,1,0:T(8,128)S(1)} %fusion.201), channel_id=1, replica_groups=mesh['scalar'=4,'space'=8] {'space'}, dimensions={0} | all-to-all | bytes 8388608 | tf_op jit(solution)/shard_map/all_to_all | solution.py:115
  492.3 4.9 bitcast_multiply_fusion
  503.3 4.6 fusion.87
  533.4 17.1 %maximum_select_fusion.101 = f32[4,2,128,1024]{2,3,1,0:T(8,128)S(1)} fusion(f32[4,2,128,1016]{2,3,1,0:T(8,128)} %get-tuple-element.6, f32[4,2,128,8]{2,3,1,0:T(8,128)S(1)} %get-tuple-element.8, f32[4,2,128,1017]{2,3,1,0:T(8,128)S(1)} %get-tuple-element.10, f32[4,2,128,7]{2,3,1,0:T(8,128)S(1)} %get-tuple-element.12, ...), kind=kLoop, calls=%fused_computation.127.clone.clone | loop fusion | flops 34603008 | bytes 75501824 | tf_op jit(solution)/shard_map/dot_general | solution.py:59
  550.4 44.2 %fusion.88 = f32[4,2,128,1024]{3,2,1,0:T(8,128)S(1)} fusion(s32[1024]{0:T(1024)S(1)} %copy-done.69, pred[1024]{0:T(1024)(128)(4,1)S(1)} %copy-done.74, f32[4,2,128,1024]{2,3,1,0:T(8,128)S(1)} %maximum_select_fusion.101), kind=kOutput, calls=%fused_computation.128 | convolution fusion | flops 12900630528 | bytes 8393728 | tf_op jit(solution)/shard_map/dot_general | solution.py:59
  595.5 32.0 %fusion.123 = f32[4,2,128,1024]{3,2,1,0:T(8,128)} fusion(f32[1024]{0:T(1024)S(1)} %copy-done.70, s32[1024]{0:T(1024)S(1)} %copy-done.69, pred[1024]{0:T(1024)(128)(4,1)S(1)} %copy-done.74, f32[4,2,128,1024]{3,2,1,0:T(8,128)S(1)} %fusion.307), kind=kOutput, calls=%fused_computation.177 | convolution fusion | flops 12901679104 | bytes 8397824 | tf_op jit(solution)/shard_map/dot_general | solution.py:64
  (276 shorter events, 174.5 us)
Async XLA Ops:
  6.5 33.1 %all-gather.3.cloned.1.call-start = ((), (), s32[]{:S(2)}) async-start(), calls=%async_computation.3 | async-start | bytes 1310720 | tf_op jit(solution)/shard_map/all_gather | solution.py:98
  7.3 100.7 %all-gather.5.cloned.1.call-start = ((), (), s32[]{:S(2)}) async-start(), calls=%async_computation.4 | async-start | bytes 1310720 | tf_op jit(solution)/shard_map/all_gather | solution.py:107
  16.8 95.1 %copy-start.35 = (pred[2,128]{1,0:T(4,128)(4,1)}, pred[2,128]{1,0:T(4,128)(4,1)S(1)}, u32[]{:S(2)}) copy-start(pred[2,128]{1,0:T(4,128)(4,1)S(1)} %get-tuple-element.142) | copy-start | bytes 772
  16.8 95.1 %copy-start.37 = (pred[2,128]{1,0:T(4,128)(4,1)}, pred[2,128]{1,0:T(4,128)(4,1)S(1)}, u32[]{:S(2)}) copy-start(pred[2,128]{1,0:T(4,128)(4,1)S(1)} %get-tuple-element.143) | copy-start | bytes 772
  16.8 95.1 %copy-start.39 = (pred[2,128]{1,0:T(4,128)(4,1)}, pred[2,128]{1,0:T(4,128)(4,1)S(1)}, u32[]{:S(2)}) copy-start(pred[2,128]{1,0:T(4,128)(4,1)S(1)} %get-tuple-element.144) | copy-start | bytes 772
  16.8 95.1 %copy-start.41 = (pred[2,128]{1,0:T(4,128)(4,1)}, pred[2,128]{1,0:T(4,128)(4,1)S(1)}, u32[]{:S(2)}) copy-start(pred[2,128]{1,0:T(4,128)(4,1)S(1)} %get-tuple-element.145) | copy-start | bytes 772
  16.8 95.1 %copy-start.43 = (pred[2,128]{1,0:T(4,128)(4,1)}, pred[2,128]{1,0:T(4,128)(4,1)S(1)}, u32[]{:S(2)}) copy-start(pred[2,128]{1,0:T(4,128)(4,1)S(1)} %get-tuple-element.146) | copy-start | bytes 772
  16.8 95.1 %copy-start.45 = (pred[2,128]{1,0:T(4,128)(4,1)}, pred[2,128]{1,0:T(4,128)(4,1)S(1)}, u32[]{:S(2)}) copy-start(pred[2,128]{1,0:T(4,128)(4,1)S(1)} %get-tuple-element.147) | copy-start | bytes 772
  16.9 95.1 %copy-start.47 = (pred[2,128]{1,0:T(4,128)(4,1)}, pred[2,128]{1,0:T(4,128)(4,1)S(1)}, u32[]{:S(2)}) copy-start(pred[2,128]{1,0:T(4,128)(4,1)S(1)} %get-tuple-element.148) | copy-start | bytes 772
  16.9 95.1 %copy-start.49 = (pred[2,128]{1,0:T(4,128)(4,1)}, pred[2,128]{1,0:T(4,128)(4,1)S(1)}, u32[]{:S(2)}) copy-start(pred[2,128]{1,0:T(4,128)(4,1)S(1)} %get-tuple-element.149) | copy-start | bytes 772
  16.9 95.1 %copy-start.51 = (pred[2,128]{1,0:T(4,128)(4,1)}, pred[2,128]{1,0:T(4,128)(4,1)S(1)}, u32[]{:S(2)}) copy-start(pred[2,128]{1,0:T(4,128)(4,1)S(1)} %get-tuple-element.150) | copy-start | bytes 772
  16.9 95.1 %copy-start.53 = (pred[2,128]{1,0:T(4,128)(4,1)}, pred[2,128]{1,0:T(4,128)(4,1)S(1)}, u32[]{:S(2)}) copy-start(pred[2,128]{1,0:T(4,128)(4,1)S(1)} %get-tuple-element.151) | copy-start | bytes 772
  16.9 95.1 %copy-start.55 = (pred[2,128]{1,0:T(4,128)(4,1)}, pred[2,128]{1,0:T(4,128)(4,1)S(1)}, u32[]{:S(2)}) copy-start(pred[2,128]{1,0:T(4,128)(4,1)S(1)} %get-tuple-element.152) | copy-start | bytes 772
  16.9 95.1 %copy-start.57 = (pred[2,128]{1,0:T(4,128)(4,1)}, pred[2,128]{1,0:T(4,128)(4,1)S(1)}, u32[]{:S(2)}) copy-start(pred[2,128]{1,0:T(4,128)(4,1)S(1)} %get-tuple-element.153) | copy-start | bytes 772
  16.9 95.1 %copy-start.59 = (pred[2,128]{1,0:T(4,128)(4,1)}, pred[2,128]{1,0:T(4,128)(4,1)S(1)}, u32[]{:S(2)}) copy-start(pred[2,128]{1,0:T(4,128)(4,1)S(1)} %get-tuple-element.154) | copy-start | bytes 772
  17.6 161.0 %copy-start.32 = (f32[4,1024]{1,0:T(4,128)}, f32[4,1024]{1,0:T(4,128)S(1)}, u32[]{:S(2)}) copy-start(f32[4,1024]{1,0:T(4,128)S(1)} %get-tuple-element.141) | copy-start | bytes 49156
  46.9 11.6 %copy-start.10 = (f32[2,128,1024]{1,2,0:T(8,128)}, f32[2,128,1024]{1,2,0:T(8,128)S(1)}, u32[]{:S(2)}) copy-start(f32[2,128,1024]{1,2,0:T(8,128)S(1)} %copy.145) | copy-start | bytes 3145732
  75.7 28.3 %copy-start = (f32[4,2,128,1024]{2,3,1,0:T(8,128)}, f32[4,2,128,1024]{2,3,1,0:T(8,128)S(1)}, u32[]{:S(2)}) copy-start(f32[4,2,128,1024]{2,3,1,0:T(8,128)S(1)} %fusion.9) | copy-start | bytes 12582916
  108.0 122.1 %all-to-all-start.1 = ((f32[1,2,128,1024]{2,1,0,3:T(2,128)}), f32[1,2,128,1024]{2,1,0,3:T(2,128)S(1)}, u32[]{:S(2)}, u32[]{:S(2)}) async-start(f32[1,2,128,1024]{2,1,0,3:T(2,128)} %bitcast.236), calls=%async_computation.1 | async-start | bytes 2097152 | tf_op jit(solution)/shard_map/all_to_all | solution.py:110
  112.1 22.5 %copy-start.69 = (s32[1024]{0:T(1024)S(1)}, s32[1024]{0:T(1024)}, u32[]{:S(2)}) copy-start(s32[1024]{0:T(1024)} %add_select_fusion.2) | copy-start | bytes 12292
  112.1 22.5 %copy-start.74 = (pred[1024]{0:T(1024)(128)(4,1)S(1)}, pred[1024]{0:T(1024)(128)(4,1)}, u32[]{:S(2)}) copy-start(pred[1024]{0:T(1024)(128)(4,1)} %iota_compare_fusion.1) | copy-start | bytes 3076
  230.1 61.6 %all-to-all-start = ((f32[4,2,128,1024]{2,1,0,3:T(2,128)}), f32[4,2,128,1024]{2,1,0,3:T(2,128)}, u32[]{:S(2)}, u32[]{:S(2)}) async-start(f32[4,2,128,1024]{2,1,0,3:T(2,128)} %copy.156), calls=%async_computation | async-start | bytes 8388608 | tf_op jit(solution)/shard_map/all_to_all | solution.py:109
  360.0 44.4 %copy-start.34 = (f32[4,1024]{1,0:T(4,128)S(1)}, f32[4,1024]{1,0:T(4,128)}, u32[]{:S(2)}) copy-start(f32[4,1024]{1,0:T(4,128)} %get-tuple-element.140) | copy-start | bytes 49156
  550.4 44.2 %copy-start.33 = (f32[4,1024]{1,0:T(4,128)S(1)}, f32[4,1024]{1,0:T(4,128)}, u32[]{:S(2)}) copy-start(f32[4,1024]{1,0:T(4,128)} %copy-done.32) | copy-start | bytes 49156
  (55 other events, 265.6 us)
Sparse Core Ops, SparseCore 0:
  8.9 30.6 all-gather.2
  41.2 27.4 all-gather.4
